TPU v7x, 128 devices: a whole 4x4x4 slice. The times are simulated.
128 devices in a mesh: src: 16 (over z_hi, x, core), snode: 8 (over y, z_lo).
Axes of the slice: x: 4, y: 4, z: 4 (z_hi: 2, z_lo: 2; z = z_hi * 2 + z_lo), core: 2. Of those that a mesh axis runs over, the one named last changes fastest.
Arguments:
- leaf_rhs: float32 [64, 256, 2048], P('snode', None, 'src'), may hold values from -6 to 6
- top_rhs: float32 [2048, 2048], P(None, 'src'), may hold values from -6 to 6
- leaf_inv: float32 [64, 256, 256], P('snode'), may hold values from -1 to 1, as said below
- coupling: float32 [64, 2048, 256], P('snode'), may hold values from -0.046875 to 0.046875
- top_inv: float32 [2048, 2048], P('snode'), may hold values from -1 to 1, as said below
- cond: float32 [64, 256], P('snode'), may hold values from 0.1 to 3
- electrodes: int32 [8192, 4], P('src'), may hold values from 0 to 2047, all different within a row
- blocks: int32 [16, 8192], P(None, 'src'), may hold values from 0 to 63
Outputs:
- sens: float32 [16, 256, 8192], P('snode', None, 'src')
Inputs may be any that keep to these rules, and one draw needn't show every extreme that they name: `electrodes`: the four sources of a row are different. `leaf_inv`: zero above the diagonal of each block. `top_inv`: zero above the diagonal.
All inputs are finite; a program needn't handle non-finite values.
Results may differ from a plain program's by a relative error of at most 0.00011.
Values sent between devices are 32-bit elements; how exact they have to be, the bound alone decides.
No kernel may reach another device: no remote copies, remote signals or barrier semaphores. Data moves between devices by JAX's collectives and lax.ppermute only.
A program may use at most 320 MiB of HBM per device.

v0:
```python
import jax
import jax.numpy as jnp
from jax import lax
from jax.sharding import PartitionSpec as P


def local(leaf_rhs, top_rhs, leaf_inv, coupling, top_inv, cond, electrodes, blocks):
    highest = lax.Precision.HIGHEST
    forward_leaf = jnp.einsum("bij,bjs->bis", leaf_inv, leaf_rhs, precision=highest)
    partial_value = jnp.einsum("bti,bis->ts", coupling, forward_leaf, precision=highest)
    coupled = lax.psum(partial_value, "snode")
    residual = top_rhs - coupled
    forward_top = jnp.dot(top_inv, residual, precision=highest)
    top_partial = jnp.einsum("rt,rs->ts", top_inv, forward_top, precision=highest)
    separator_field = lax.psum(top_partial, "snode")
    adjusted = forward_leaf - jnp.einsum(
        "bti,ts->bis", coupling, separator_field, precision=highest
    )
    leaf_field = jnp.einsum("bji,bjs->bis", leaf_inv, adjusted, precision=highest)
    leaves = leaf_field.shape[0]
    cells_n = leaf_field.shape[1]
    quads_n = electrodes.shape[0]
    shard_piece = lax.all_gather(leaf_field, "src", axis=2, tiled=True)
    width_n = shard_piece.shape[2]
    source_ids = lax.broadcasted_iota(jnp.int32, (width_n, quads_n), 0)

    def signed(plus_ids, minus_ids):
        upper = (source_ids == plus_ids[None, :]).astype(jnp.float32)
        lower = (source_ids == minus_ids[None, :]).astype(jnp.float32)
        return upper - lower

    current_sel = signed(electrodes[:, 0], electrodes[:, 1])
    potential_sel = signed(electrodes[:, 2], electrodes[:, 3])
    current_add = jnp.einsum("bcs,sq->bcq", shard_piece, current_sel, precision=highest)
    potential_add = jnp.einsum("bcs,sq->bcq", shard_piece, potential_sel, precision=highest)
    product = current_add * potential_add
    weighted = cond[:, :, None] * product
    owner_id = lax.axis_index("snode")
    local_blocks = blocks - owner_id * leaves
    own_rows = blocks.shape[0] // lax.axis_size("snode")
    summed = jnp.zeros((own_rows * lax.axis_size("snode"), cells_n, quads_n), jnp.float32)
    for leaf_id in range(leaves):
        summed = summed + jnp.where(
            (local_blocks == leaf_id)[:, None, :], weighted[leaf_id][None], 0.0
        )
    return lax.psum_scatter(summed, "snode", scatter_dimension=0, tiled=True)


def solution(mesh):
    return jax.shard_map(
        local,
        mesh=mesh,
        in_specs=(
            P("snode", None, "src"),
            P(None, "src"),
            P("snode", None, None),
            P("snode", None, None),
            P("snode", None),
            P("snode", None),
            P("src", None),
            P(None, "src"),
        ),
        out_specs=P("snode", None, "src"),
        check_vma=False,
    )
```

profile of v0, /device:TPU:1, one launch (start us, length us, event | category | flops | bytes accessed | tf_op | source)
XLA Modules:
  0.0 582.9 jit_solution(11139085248551137085)
XLA Ops:
  6.5 0.0 copy-start
  6.5 0.0 all-reduce.3.cloned.1.call-start
  6.5 1.6 copy-done
  8.1 3.2 fusion.21
  11.3 17.3 %convolution_bitcast_fusion = f32[2048,128]{1,0:T(8,128)} fusion(f32[8,256,128]{2,1,0:T(8,128)S(1)} %fusion.21, f32[8,2048,256]{2,1,0:T(8,128)} %param.11), kind=kOutput, calls=%fused_computation.16 | convolution fusion | flops 6442450944 | bytes 18874368 | tf_op jit(solution)/shard_map/bti,bis->ts/dot_general | solution.py:10
  28.6 0.0 all-reduce.3.cloned.1.call-update
  28.6 0.0 all-reduce.5.cloned.1.call-start
  28.6 76.9 %all-reduce.3.cloned.1.call-done = f32[2048,128]{1,0:T(8,128)} async-done(((f32[2048,128]{1,0:T(8,128)}), f32[2048,128]{1,0:T(8,128)}) %all-reduce.3.cloned.1.call-update) | async-done | bytes 1048592 | tf_op jit(solution)/shard_map/psum | solution.py:11
  105.5 0.0 copy-start.2
  105.6 4.2 fusion.18
  109.8 0.0 copy-done.2
  109.8 2.2 convolution_bitcast_fusion.1
  112.0 0.0 all-reduce.5.cloned.1.call-update
  112.0 0.3 all-gather.2.cloned.1.call-start
  112.3 77.3 %all-reduce.5.cloned.1.call-done = f32[2048,128]{0,1:T(8,128)} async-done(((f32[2048,128]{0,1:T(8,128)}), f32[2048,128]{0,1:T(8,128)}) %all-reduce.5.cloned.1.call-update) | async-done | bytes 1048592 | tf_op jit(solution)/shard_map/psum | solution.py:15
  189.6 29.2 %fusion.16 = f32[8,256,128]{2,1,0:T(8,128)S(1)} fusion(f32[8,256,128]{2,1,0:T(8,128)S(1)} %fusion.21, f32[8,2048,256]{2,1,0:T(8,128)} %param.11, f32[2048,128]{0,1:T(8,128)} %all-reduce.5.cloned.1.call-done), kind=kOutput, calls=%fused_computation.24 | convolution fusion | flops 6442713088 | bytes 19922944 | tf_op jit(solution)/shard_map/bti,ts->bis/dot_general | solution.py:16
  218.8 0.0 copy-start.4
  218.9 0.0 copy-start.3
  218.9 3.0 convolution_bitcast_fusion.2
  221.9 0.0 all-gather.2.cloned.1.call-update
  221.9 0.6 reduce-scatter.2.cloned.1.call-start
  222.5 0.0 copy-done.4
  222.5 0.0 copy-done.3
  222.6 113.9 %all-gather.2.cloned.1.call-done = f32[8,256,2048]{1,2,0:T(8,128)} async-done(((f32[8,256,128]{1,2,0:T(8,128)}), f32[8,256,2048]{1,2,0:T(8,128)}) %all-gather.2.cloned.1.call-update) | async-done | bytes 16777232 | tf_op jit(solution)/shard_map/all_gather | solution.py:23
  336.5 0.0 copy-start.5
  336.5 0.0 copy-start.6
  336.5 32.1 %fusion = f32[8,256,512]{2,1,0:T(8,128)S(1)} fusion(f32[8,256,2048]{1,2,0:T(8,128)} %all-gather.2.cloned.1.call-done, s32[512]{0:T(512)S(1)} %bitcast.57, s32[512]{0:T(512)S(1)} %bitcast.58), kind=kOutput, calls=%fused_computation.1 | convolution fusion | flops 25775046656 | bytes 20975616 | tf_op jit(solution)/shard_map/bcs,sq->bcq/dot_general | solution.py:35
  368.6 0.0 copy-done.5
  368.6 0.0 copy-done.6
  368.6 30.3 %multiply_multiply_fusion = f32[8,256,512]{2,1,0:T(8,128)S(1)} fusion(f32[8,256,512]{2,1,0:T(8,128)S(1)} %fusion, f32[8,256,2048]{1,2,0:T(8,128)S(1)} %copy-done.5, s32[512]{0:T(512)S(1)} %bitcast.56, s32[512]{0:T(512)S(1)} %bitcast.55, f32[8,256]{1,0:T(8,128)S(1)} %copy-done.6), kind=kOutput, calls=%fused_computation.5 | convolution fusion | flops 25777143808 | bytes 25178112 | tf_op jit(solution)/shard_map/bcs,sq->bcq/dot_general | solution.py:34
  398.9 0.5 slice_bitcast_fusion.7
  399.3 10.2 %select_add_fusion = f32[16,256,512]{2,1,0:T(8,128)} fusion(f32[256,512]{1,0:T(8,128)S(1)} %get-tuple-element.6, f32[256,512]{1,0:T(8,128)S(1)} %get-tuple-element.7, f32[256,512]{1,0:T(8,128)S(1)} %get-tuple-element.8, f32[256,512]{1,0:T(8,128)S(1)} %get-tuple-element.9, f32[256,512]{1,0:T(8,128)S(1)} %get-tuple-element.10, ...), kind=kLoop, calls=%fused_computation | loop fusion | flops 31457280 | bytes 12648448 | tf_op jit(solution)/shard_map/add | solution.py:43
  409.5 0.0 copy-start.1
  409.5 0.0 reduce-scatter.2.cloned.1.call-update
  409.5 166.6 %reduce-scatter.2.cloned.1.call-done = f32[2,256,512]{2,1,0:T(8,128)} async-done(((f32[16,256,512]{2,1,0:T(8,128)}), f32[2,256,512]{2,1,0:T(8,128)}) %reduce-scatter.2.cloned.1.call-update) | async-done | bytes 1048592 | tf_op jit(solution)/shard_map/reduce_scatter | solution.py:46
  576.1 0.0 copy-done.1
  (2 shorter events, 0.1 us)
Async XLA Ops:
  6.5 1.6 copy-start
  6.5 99.0 %all-reduce.3.cloned.1.call-start = ((), (), s32[]{:S(2)}) async-start(), calls=%async_computation.1 | async-start | bytes 2097152 | tf_op jit(solution)/shard_map/psum | solution.py:11
  28.6 161.1 %all-reduce.5.cloned.1.call-start = ((), (), s32[]{:S(2)}) async-start(), calls=%async_computation.2 | async-start | bytes 2097152 | tf_op jit(solution)/shard_map/psum | solution.py:15
  105.5 4.2 copy-start.2
  112.0 224.5 %all-gather.2.cloned.1.call-start = ((), (), s32[]{:S(2)}) async-start(), calls=%async_computation.3 | async-start | bytes 17825792 | tf_op jit(solution)/shard_map/all_gather | solution.py:23
  218.8 3.6 copy-start.4
  218.9 3.6 copy-start.3
  221.9 354.2 %reduce-scatter.2.cloned.1.call-start = ((), (), s32[]{:S(2)}) async-start(), calls=%async_computation.4 | async-start | bytes 9437184 | tf_op jit(solution)/shard_map/reduce_scatter | solution.py:46
  336.5 32.1 %copy-start.5 = (f32[8,256,2048]{1,2,0:T(8,128)S(1)}, f32[8,256,2048]{1,2,0:T(8,128)}, u32[]{:S(2)}) copy-start(f32[8,256,2048]{1,2,0:T(8,128)} %all-gather.2.cloned.1.call-done) | copy-start | bytes 50331652
  336.5 32.1 %copy-start.6 = (f32[8,256]{1,0:T(8,128)S(1)}, f32[8,256]{1,0:T(8,128)}, u32[]{:S(2)}) copy-start(f32[8,256]{1,0:T(8,128)} %param.13) | copy-start | bytes 24580
  409.5 166.6 %copy-start.1 = (f32[8,256,256]{2,1,0:T(8,128)S(1)}, f32[8,256,256]{2,1,0:T(8,128)}, u32[]{:S(2)}) copy-start(f32[8,256,256]{2,1,0:T(8,128)} %param.10) | copy-start | bytes 6291460
Sparse Core Ops, SparseCore 0:
  28.7 76.7 all-reduce.2
  112.1 77.4 all-reduce.4
  222.0 114.4 all-gather.1
  409.7 166.3 reduce-scatter.1
where the time goes:
time: 590 us; the launch traced here: 583 us
  waiting for transfers between devices  435 us (74%)
  matrix products  121 us (21%)
  between operations  13.5 us (2%)
  other arithmetic  10.2 us (2%)
    reduce_scatter x1, waiting for transfers between devices, local(): return lax.psum_scatter(summed, 'snode', scatter_dimension=0, tiled=True)  167 us
    all_gather x1, waiting for transfers between devices, local(): shard_piece = lax.all_gather(leaf_field, 'src', axis=2, tiled=True)  114 us
    psum x1, waiting for transfers between devices, local(): separator_field = lax.psum(top_partial, 'snode')  77.3 us
    psum x1, waiting for transfers between devices, local(): coupled = lax.psum(partial_value, 'snode')  76.9 us
    dot_general x1, matrix products, local(): jnp.einsum('bcs,sq->bcq', shard_piece, potential_sel, precision=highest)  32.1 us
    dot_general x1, matrix products, local(): jnp.einsum('bcs,sq->bcq', shard_piece, current_sel, precision=highest)  30.3 us
    dot_general x1, matrix products, local(): jnp.einsum('bti,ts->bis', coupling, separator_field, precision=highest)  29.2 us
    dot_general x1, matrix products, local(): jnp.einsum('bti,bis->ts', coupling, forward_leaf, precision=highest)  17.3 us
  transfers between devices with their start and end apart: 4, of which 4 were waited for; matrix products, arithmetic and copies ran while one was open for 0% of the time, Pallas kernels for 0%

commit v1 on v0

--- a/solution.py
+++ b/solution.py
@@ -20,7 +20,9 @@
     leaves = leaf_field.shape[0]
     cells_n = leaf_field.shape[1]
     quads_n = electrodes.shape[0]
-    shard_piece = lax.all_gather(leaf_field, "src", axis=2, tiled=True)
+    shard_piece = jnp.concatenate(
+        lax.all_to_all(jnp.stack([leaf_field] * lax.axis_size("src")), "src", 0, 0), axis=2
+    )
     width_n = shard_piece.shape[2]
     source_ids = lax.broadcasted_iota(jnp.int32, (width_n, quads_n), 0)
 

time: 590 us -> 723 us (1.23)
  waiting for transfers between devices: 435 us -> 548 us
  starting transfers between devices: 0.94 us -> 11.5 us
  local copies, waits for them, and re-layouts: 2.08 us -> 10.3 us
    all_to_all x0 -> x1, waiting for transfers between devices: none -> 224 us  [local(): lax.all_to_all(jnp.stack([leaf_field] * lax.axis_size('src')), 'src', 0, 0)]
    all_gather x1 -> x0, waiting for transfers between devices: 114 us -> none  [local(): shard_piece = lax.all_gather(leaf_field, 'src', axis=2, tiled=True)]
    all_to_all x0 -> x1, starting transfers between devices: none -> 11.4 us  [local(): lax.all_to_all(jnp.stack([leaf_field] * lax.axis_size('src')), 'src', 0, 0)]
    another operation x0 -> x1, local copies, waits for them, and re-layouts: none -> 7.91 us  [local(): jnp.stack([leaf_field] * lax.axis_size('src'))]
where the time goes in v1:
time: 723 us; the launch traced here: 716 us
  waiting for transfers between devices  548 us (76%)
  matrix products  123 us (17%)
  between operations  13.5 us (2%)
  starting transfers between devices  11.5 us (2%)
  local copies, waits for them, and re-layouts  10.3 us (1%)
  other arithmetic  10 us (1%)
    all_to_all x1, waiting for transfers between devices, local(): lax.all_to_all(jnp.stack([leaf_field] * lax.axis_size('src')), 'src', 0, 0)  224 us
    reduce_scatter x1, waiting for transfers between devices, local(): return lax.psum_scatter(summed, 'snode', scatter_dimension=0, tiled=True)  169 us
    psum x1, waiting for transfers between devices, local(): separator_field = lax.psum(top_partial, 'snode')  77.6 us
    psum x1, waiting for transfers between devices, local(): coupled = lax.psum(partial_value, 'snode')  76.9 us
    dot_general x1, matrix products, local(): jnp.einsum('bcs,sq->bcq', shard_piece, current_sel, precision=highest)  32.5 us
    dot_general x1, matrix products, local(): jnp.einsum('bcs,sq->bcq', shard_piece, potential_sel, precision=highest)  32.4 us
    dot_general x1, matrix products, local(): jnp.einsum('bti,ts->bis', coupling, separator_field, precision=highest)  29.6 us
    dot_general x1, matrix products, local(): jnp.einsum('bti,bis->ts', coupling, forward_leaf, precision=highest)  17.3 us
  transfers between devices with their start and end apart: 4, of which 4 were waited for; matrix products, arithmetic and copies ran while one was open for 0% of the time, Pallas kernels for 0%

profile of v1, /device:TPU:1, one launch (start us, length us, event | category | flops | bytes accessed | tf_op | source)
XLA Modules:
  0.0 716.2 jit_solution(14421967778257465576)
XLA Ops:
  6.5 0.0 copy-start
  6.5 0.0 all-reduce.3.cloned.1.call-start
  6.5 1.6 copy-done
  8.1 3.2 fusion.27
  11.3 17.3 %convolution_bitcast_fusion = f32[2048,128]{1,0:T(8,128)} fusion(f32[8,256,128]{2,1,0:T(8,128)S(1)} %fusion.27, f32[8,2048,256]{2,1,0:T(8,128)} %param.11), kind=kOutput, calls=%fused_computation.20 | convolution fusion | flops 6442450944 | bytes 18874368 | tf_op jit(solution)/shard_map/bti,bis->ts/dot_general | solution.py:10
  28.6 0.0 all-reduce.3.cloned.1.call-update
  28.6 0.0 all-reduce.5.cloned.1.call-start
  28.6 76.9 %all-reduce.3.cloned.1.call-done = f32[2048,128]{1,0:T(8,128)} async-done(((f32[2048,128]{1,0:T(8,128)}), f32[2048,128]{1,0:T(8,128)}) %all-reduce.3.cloned.1.call-update) | async-done | bytes 1048592 | tf_op jit(solution)/shard_map/psum | solution.py:11
  105.5 0.0 copy-start.2
  105.6 4.2 fusion.24
  109.8 0.0 copy-done.2
  109.8 2.2 convolution_bitcast_fusion.1
  112.0 0.0 all-reduce.5.cloned.1.call-update
  112.0 77.6 %all-reduce.5.cloned.1.call-done = f32[2048,128]{0,1:T(8,128)} async-done(((f32[2048,128]{0,1:T(8,128)}), f32[2048,128]{0,1:T(8,128)}) %all-reduce.5.cloned.1.call-update) | async-done | bytes 1048592 | tf_op jit(solution)/shard_map/psum | solution.py:15
  189.6 29.6 %fusion.22 = f32[8,256,128]{2,1,0:T(8,128)S(1)} fusion(f32[8,256,128]{2,1,0:T(8,128)S(1)} %fusion.27, f32[8,2048,256]{2,1,0:T(8,128)} %param.11, f32[2048,128]{0,1:T(8,128)} %all-reduce.5.cloned.1.call-done), kind=kOutput, calls=%fused_computation.28 | convolution fusion | flops 6442713088 | bytes 19922944 | tf_op jit(solution)/shard_map/bti,ts->bis/dot_general | solution.py:16
  219.3 2.0 convolution_bitcast_fusion.2
  221.3 0.3 copy.12
  221.7 7.9 %stack.2 = f32[16,8,256,128]{3,2,1,0:T(8,128)} broadcast(f32[8,256,128]{2,1,0:T(8,128)S(1)} %copy.12), dimensions={1,2,3} | broadcast | bytes 17825792 | tf_op jit(solution)/shard_map/stack | solution.py:24
  229.6 0.0 copy-start.4
  229.6 0.0 copy-start.3
  229.6 11.4 %all-to-all-start = ((f32[16,8,256,128]{3,2,1,0:T(8,128)}), f32[16,8,256,128]{3,2,1,0:T(8,128)}, u32[]{:S(2)}, u32[]{:S(2)}) async-start(f32[16,8,256,128]{3,2,1,0:T(8,128)} %stack.2), calls=%async_computation | async-start | bytes 33554432 | tf_op jit(solution)/shard_map/all_to_all | solution.py:24
  241.0 0.0 reduce-scatter.2.cloned.1.call-start
  241.1 0.0 copy-done.4
  241.1 0.0 copy-done.3
  241.2 224.3 %all-to-all-done = f32[16,8,256,128]{3,2,1,0:T(8,128)} async-done(((f32[16,8,256,128]{3,2,1,0:T(8,128)}), f32[16,8,256,128]{3,2,1,0:T(8,128)}, u32[]{:S(2)}, u32[]{:S(2)}) %all-to-all-start) | async-done | bytes 16777248 | tf_op jit(solution)/shard_map/all_to_all | solution.py:24
  465.5 0.0 copy-start.5
  465.5 32.4 %fusion = f32[8,256,512]{2,1,0:T(8,128)S(1)} fusion(s32[512]{0:T(512)S(1)} %bitcast.70, s32[512]{0:T(512)S(1)} %bitcast.71, f32[16,8,256,128]{3,2,1,0:T(8,128)} %all-to-all-done), kind=kOutput, calls=%fused_computation | convolution fusion | flops 25775046656 | bytes 20975616 | tf_op jit(solution)/shard_map/bcs,sq->bcq/dot_general | solution.py:37
  497.9 0.0 copy-done.5
  497.9 32.5 %multiply_multiply_fusion = f32[8,256,512]{2,1,0:T(8,128)S(1)} fusion(f32[8,256,512]{2,1,0:T(8,128)S(1)} %fusion, s32[512]{0:T(512)S(1)} %bitcast.69, s32[512]{0:T(512)S(1)} %bitcast.68, f32[8,256]{1,0:T(8,128)S(1)} %copy-done.5, f32[16,8,256,128]{3,2,1,0:T(8,128)} %all-to-all-done), kind=kOutput, calls=%fused_computation.9 | convolution fusion | flops 25777143808 | bytes 25178112 | tf_op jit(solution)/shard_map/bcs,sq->bcq/dot_general | solution.py:36
  530.4 0.5 slice_bitcast_fusion.7
  530.8 10.0 %select_add_fusion = f32[16,256,512]{2,1,0:T(8,128)} fusion(f32[256,512]{1,0:T(8,128)S(1)} %get-tuple-element.6, f32[256,512]{1,0:T(8,128)S(1)} %get-tuple-element.7, f32[256,512]{1,0:T(8,128)S(1)} %get-tuple-element.8, f32[256,512]{1,0:T(8,128)S(1)} %get-tuple-element.9, f32[256,512]{1,0:T(8,128)S(1)} %get-tuple-element.10, ...), kind=kLoop, calls=%fused_computation.6 | loop fusion | flops 31457280 | bytes 12648448 | tf_op jit(solution)/shard_map/add | solution.py:45
  540.8 0.0 copy-start.1
  540.8 0.0 reduce-scatter.2.cloned.1.call-update
  540.8 168.6 %reduce-scatter.2.cloned.1.call-done = f32[2,256,512]{2,1,0:T(8,128)} async-done(((f32[16,256,512]{2,1,0:T(8,128)}), f32[2,256,512]{2,1,0:T(8,128)}) %reduce-scatter.2.cloned.1.call-update) | async-done | bytes 1048592 | tf_op jit(solution)/shard_map/reduce_scatter | solution.py:48
  709.4 0.0 copy-done.1
  (2 shorter events, 0.1 us)
Async XLA Ops:
  6.5 1.6 copy-start
  6.5 99.0 %all-reduce.3.cloned.1.call-start = ((), (), s32[]{:S(2)}) async-start(), calls=%async_computation.2 | async-start | bytes 2097152 | tf_op jit(solution)/shard_map/psum | solution.py:11
  28.6 161.1 %all-reduce.5.cloned.1.call-start = ((), (), s32[]{:S(2)}) async-start(), calls=%async_computation.3 | async-start | bytes 2097152 | tf_op jit(solution)/shard_map/psum | solution.py:15
  105.5 4.2 copy-start.2
  229.6 11.5 %copy-start.4 = (s32[512,4]{0,1:T(4,128)S(1)}, s32[512,4]{0,1:T(4,128)}, u32[]{:S(2)}) copy-start(s32[512,4]{0,1:T(4,128)} %param.14) | copy-start | bytes 24580
  229.6 11.5 %copy-start.3 = (s32[16,512]{1,0:T(8,128)S(1)}, s32[16,512]{1,0:T(8,128)}, u32[]{:S(2)}) copy-start(s32[16,512]{1,0:T(8,128)} %param.15) | copy-start | bytes 98308
  229.6 235.9 %all-to-all-start = ((f32[16,8,256,128]{3,2,1,0:T(8,128)}), f32[16,8,256,128]{3,2,1,0:T(8,128)}, u32[]{:S(2)}, u32[]{:S(2)}) async-start(f32[16,8,256,128]{3,2,1,0:T(8,128)} %stack.2), calls=%async_computation | async-start | bytes 33554432 | tf_op jit(solution)/shard_map/all_to_all | solution.py:24
  241.0 468.4 %reduce-scatter.2.cloned.1.call-start = ((), (), s32[]{:S(2)}) async-start(), calls=%async_computation.4 | async-start | bytes 9437184 | tf_op jit(solution)/shard_map/reduce_scatter | solution.py:48
  465.5 32.4 %copy-start.5 = (f32[8,256]{1,0:T(8,128)S(1)}, f32[8,256]{1,0:T(8,128)}, u32[]{:S(2)}) copy-start(f32[8,256]{1,0:T(8,128)} %param.13) | copy-start | bytes 24580
  540.8 168.6 %copy-start.1 = (f32[8,256,256]{2,1,0:T(8,128)S(1)}, f32[8,256,256]{2,1,0:T(8,128)}, u32[]{:S(2)}) copy-start(f32[8,256,256]{2,1,0:T(8,128)} %param.10) | copy-start | bytes 6291460
Sparse Core Ops, SparseCore 0:
  28.7 76.7 all-reduce.2
  112.1 77.4 all-reduce.4
  541.0 168.4 reduce-scatter.1
